TPU v7x, 32 devices: a whole 2x2x4 slice. The times are simulated.
32 devices in a mesh: dom: 2 (over x), store: 8 (over z, y), mp: 2 (over core).
Axes of the slice: x: 2, y: 2, z: 4, core: 2. Of those that a mesh axis runs over, the one named last changes fastest.
Arguments:
- layer_input: bfloat16 [16, 512, 8192], P('dom', 'store', 'mp'), parts along dimension 0, may hold values from -6 to 6
- out_grad: bfloat16 [16, 512, 8192], P('dom', 'store', 'mp'), parts along dimension 0, may hold values from -6 to 6
- proj_in: bfloat16 [64, 8192], P(None, 'mp'), may hold values from -0.0625 to 0.0625
- proj_out: bfloat16 [64, 8192], P(None, 'mp'), may hold values from -0.0625 to 0.0625
- counts: int32 [16], P('dom'), parts along dimension 0, may hold values from 256 to 512, as said below
- store_rows: bfloat16 [12288, 4096], P(('dom', 'store', 'mp')), parts along dimension 0, may hold values from -6 to 6
- doc_ids: int32 [12288], P(('dom', 'store', 'mp')), parts along dimension 0, may hold values from 0 to 191, never falling along the last dimension, each value on 1 to 64 neighbouring positions
Outputs:
- query_grads: float32 [16, 4096], P('dom'), parts along dimension 0
- row_scores: float32 [16, 6144], P('dom', ('store', 'mp')), parts along dimension 0
- doc_scores: float32 [16, 6144], P('dom', ('store', 'mp')), parts along dimension 0
There are 2 independent parts, one for each index of `dom`. A program takes and returns all parts, laid end to end along the dimension named above; an argument that names none is the same for every part. Nothing has to cross between parts.
Inputs may be any that keep to these rules, and one draw needn't show every extreme that they name: `counts`: some query example has exactly 512 real tokens and some exactly 256. `doc_ids`: each dom group numbers its own training examples from 0 to 191. Within one group the rows of one training example are consecutive, ids never fall along the rows, and one example has exactly 64 rows.
All inputs are finite; a program needn't handle non-finite values.
Results may differ from a plain program's by a relative error of at most 0.0029.
Values sent between devices are 32-bit elements; how exact they have to be, the bound alone decides.
A program may use at most 64 MiB of HBM per device.

v0:
```python
import jax
import jax.numpy as jnp
from jax import lax
from jax.sharding import PartitionSpec as P


def padded_2(value, sides, width):
    for axis, dim in sides:
        count, length = (lax.axis_size(axis), value.shape[dim])
        up = [(i, (i + 1) % count) for i in range(count - 1)]
        down = [(j, i) for i, j in up]
        last = lax.slice_in_dim(value, length - width, length, axis=dim)
        first = lax.slice_in_dim(value, 0, width, axis=dim)
        before = lax.ppermute(last, axis, up)
        after = lax.ppermute(first, axis, down)
        value = jnp.concatenate([before, value, after], axis=dim)
    return value


def local(layer_input, out_grad, proj_in, proj_out, counts, store_rows, doc_ids):
    query_count = layer_input.shape[0]
    seq_span = layer_input.shape[1]
    in_rank = proj_in.shape[0]
    out_rank = proj_out.shape[0]
    in_part = jnp.einsum("qtd,kd->qtk", layer_input, proj_in, preferred_element_type=jnp.float32)
    out_part = jnp.einsum("qtd,kd->qtk", out_grad, proj_out, preferred_element_type=jnp.float32)
    factors = jnp.concatenate([in_part, out_part], axis=2)
    first_pos = lax.axis_index("store") * seq_span
    summed = lax.psum(factors, "mp")
    positions = first_pos + lax.broadcasted_iota(jnp.int32, (query_count, summed.shape[1]), 1)
    token_weight = jnp.where(
        positions < counts[:, None], jnp.float32(1.0), jnp.float32(0.0)
    ) / counts[:, None].astype(jnp.float32)
    in_factor = summed[:, :, :in_rank]
    weighted = summed[:, :, in_rank:] * token_weight[:, :, None]
    partial_grads = jnp.einsum(
        "qto,qti->qoi", weighted, in_factor, precision=lax.Precision.HIGHEST
    ).reshape(query_count, out_rank * in_rank)
    query_grads = lax.psum(partial_grads, "store")
    grads_low = query_grads.astype(jnp.bfloat16)
    row_scores = lax.dot_general(
        grads_low, store_rows, (((1,), (1,)), ((), ())), preferred_element_type=jnp.float32
    )
    ids_float = doc_ids.astype(jnp.float32)
    same_doc = jnp.where(doc_ids[:, None] == doc_ids[None, :], jnp.float32(1.0), jnp.float32(0.0))
    local_total = jnp.dot(row_scores, same_doc, precision=lax.Precision.HIGHEST)
    head_entry = jnp.concatenate([ids_float[:1], local_total[:, 0]])
    tail_entry = jnp.concatenate([ids_float[-1:], local_total[:, -1]])
    summary = jnp.stack([head_entry, tail_entry])
    padded = padded_2(summary, ((("store", "mp"), 0),), 1)
    left_id = padded[0, 0]
    left_vals = padded[0, 1:]
    right_id = padded[3, 0]
    right_vals = padded[3, 1:]
    doc_scores = local_total + jnp.where(
        ids_float[None, :] == left_id, left_vals[:, None], jnp.float32(0.0)
    )
    doc_scores = doc_scores + jnp.where(
        ids_float[None, :] == right_id, right_vals[:, None], jnp.float32(0.0)
    )
    return (query_grads, row_scores, doc_scores)


def solution(mesh):
    placed = (
        P("dom", "store", "mp"),
        P("dom", "store", "mp"),
        P(None, "mp"),
        P(None, "mp"),
        P("dom"),
        P(("dom", "store", "mp"), None),
        P(("dom", "store", "mp")),
    )
    return jax.shard_map(
        local,
        mesh=mesh,
        in_specs=placed,
        out_specs=(P("dom", None), P("dom", ("store", "mp")), P("dom", ("store", "mp"))),
        check_vma=False,
    )
```

profile of v0, /device:TPU:0, one launch (start us, length us, event | category | flops | bytes accessed | tf_op | source)
XLA Modules:
  0.0 127.9 jit_solution(4479775280024926264)
XLA Ops:
  7.2 3.7 %fusion.3 = f32[8,64,64]{2,1,0:T(8,128)S(1)} fusion(bf16[8,64,4096]{2,1,0:T(8,128)(2,1)} %param.8, bf16[64,4096]{1,0:T(8,128)(2,1)} %param.10), kind=kOutput, calls=%fused_computation.3 | convolution fusion | flops 268435456 | bytes 4849664 | tf_op jit(solution)/shard_map/qtd,kd->qtk/dot_general | solution.py:26
  10.9 0.0 copy-done.4
  11.0 0.1 copy-done.5
  11.1 1.2 fusion.5
  12.3 0.8 pad_maximum_fusion
  13.2 0.0 all-reduce.5.cloned.1.call-start
  13.3 0.1 select_divide_fusion
  13.4 21.0 %all-reduce.3.cloned.1.call-done = f32[8,64,128]{2,1,0:T(8,128)} async-done(((f32[8,64,128]{2,1,0:T(8,128)}), f32[8,64,128]{2,1,0:T(8,128)}) %all-reduce.3.cloned.1.call-update) | async-done | bytes 262160 | tf_op jit(solution)/shard_map/psum | solution.py:29
  34.3 1.8 %fusion.11 = f32[8,64,64]{2,1,0:T(8,128)S(1)} fusion(f32[8,64,128]{2,1,0:T(8,128)} %all-reduce.3.cloned.1.call-done, f32[8,64]{1,0:T(8,128)S(1)} %select_divide_fusion), kind=kOutput, calls=%fused_computation.11 | convolution fusion | flops 25198592 | bytes 657408 | tf_op jit(solution)/shard_map/qto,qti->qoi/dot_general | solution.py:36
  36.1 0.8 reshape.60
  36.9 0.6 fusion.18
  37.5 71.9 %all-reduce.5.cloned.1.call-done = f32[8,4096]{1,0:T(8,128)} async-done(((f32[8,4096]{1,0:T(8,128)}), f32[8,4096]{1,0:T(8,128)}) %all-reduce.5.cloned.1.call-update) | async-done | bytes 131088 | tf_op jit(solution)/shard_map/psum | solution.py:39
  109.4 1.8 %fusion.14 = f32[8,384]{1,0:T(8,128)S(1)} fusion(bf16[384,4096]{1,0:T(8,128)(2,1)S(1)} %copy-done, f32[8,4096]{1,0:T(8,128)} %all-reduce.5.cloned.1.call-done), kind=kOutput, calls=%fused_computation.16 | convolution fusion | flops 25198592 | bytes 3289088 | tf_op jit(solution)/shard_map/dot_general | solution.py:41
  111.2 0.5 fusion
  111.7 0.2 slice_reduce_fusion.1
  111.9 0.7 maximum_bitcast_fusion
  112.7 1.3 collective-permute-start
  113.9 0.6 maximum_bitcast_fusion.1
  114.6 1.3 %collective-permute-start.1 = (f32[1,9]{1,0:T(1,128)S(1)}, f32[1,9]{1,0:T(1,128)S(1)}, u32[]{:S(2)}, u32[]{:S(2)}) collective-permute-start(f32[1,9]{1,0:T(1,128)S(1)} %maximum_bitcast_fusion.1), channel_id=1, source_target_pairs={{1,0},{2,1},{3,2},{4,3},{5,4},{6,5},{7,6},{8,7},{9,8},{10,9},{11,1... | collective-permute-start | bytes 116 | tf_op jit(solution)/shard_map/ppermute | solution.py:15
  115.9 2.7 %collective-permute-done.1 = f32[1,9]{1,0:T(1,128)S(1)} collective-permute-done((f32[1,9]{1,0:T(1,128)S(1)}, f32[1,9]{1,0:T(1,128)S(1)}, u32[]{:S(2)}, u32[]{:S(2)}) %collective-permute-start.1) | collective-permute-done | bytes 68 | tf_op jit(solution)/shard_map/ppermute | solution.py:15
  118.6 0.1 slice_bitcast_fusion
  118.7 0.1 slice_bitcast_fusion.1
  118.8 0.7 select_add_fusion
  119.5 1.6 %copy.15 = f32[8,4096]{1,0:T(8,128)} copy(f32[8,4096]{1,0:T(8,128)} %all-reduce.5.cloned.1.call-done) | data formatting | bytes 262144
  (18 shorter events, 0.1 us)
Async XLA Ops:
  7.2 102.2 %copy-start = (bf16[384,4096]{1,0:T(8,128)(2,1)S(1)}, bf16[384,4096]{1,0:T(8,128)(2,1)}, u32[]{:S(2)}) copy-start(bf16[384,4096]{1,0:T(8,128)(2,1)} %param.12) | copy-start | bytes 9437188
  7.2 27.1 %all-reduce.3.cloned.1.call-start = ((), (), s32[]{:S(2)}) async-start(), calls=%async_computation | async-start | bytes 524288 | tf_op jit(solution)/shard_map/psum | solution.py:29
  7.2 3.8 %copy-start.4 = (bf16[8,64,4096]{2,1,0:T(8,128)(2,1)S(1)}, bf16[8,64,4096]{2,1,0:T(8,128)(2,1)}, u32[]{:S(2)}) copy-start(bf16[8,64,4096]{2,1,0:T(8,128)(2,1)} %param.7) | copy-start | bytes 12582916
  7.2 3.9 %copy-start.5 = (bf16[64,4096]{1,0:T(8,128)(2,1)S(1)}, bf16[64,4096]{1,0:T(8,128)(2,1)}, u32[]{:S(2)}) copy-start(bf16[64,4096]{1,0:T(8,128)(2,1)} %param.9) | copy-start | bytes 1572868
  11.1 2.2 %copy-start.3 = (s32[8]{0:T(128)S(1)}, s32[8]{0:T(128)}, u32[]{:S(2)}) copy-start(s32[8]{0:T(128)} %param.11) | copy-start | bytes 100
  11.1 25.8 %copy-start.2 = (s32[384]{0:T(512)S(1)}, s32[384]{0:T(512)}, u32[]{:S(2)}) copy-start(s32[384]{0:T(512)} %param.13) | copy-start | bytes 4612
  13.2 96.2 %all-reduce.5.cloned.1.call-start = ((), (), s32[]{:S(2)}) async-start(), calls=%async_computation.1 | async-start | bytes 262144 | tf_op jit(solution)/shard_map/psum | solution.py:39
  111.2 9.8 %copy-start.1 = (f32[8,384]{1,0:T(8,128)}, f32[8,384]{1,0:T(8,128)S(1)}, u32[]{:S(2)}) copy-start(f32[8,384]{1,0:T(8,128)S(1)} %fusion.14) | copy-start | bytes 36868
  112.7 3.2 %collective-permute-start = (f32[1,9]{1,0:T(1,128)S(1)}, f32[1,9]{1,0:T(1,128)S(1)}, u32[]{:S(2)}, u32[]{:S(2)}) collective-permute-start(f32[1,9]{1,0:T(1,128)S(1)} %maximum_bitcast_fusion), channel_id=1, source_target_pairs={{0,1},{1,2},{2,3},{3,4},{4,5},{5,6},{6,7},{7,8},{8,9},{9,10},{10,1... | collective-permute-start | bytes 116 | tf_op jit(solution)/shard_map/ppermute | solution.py:14
  114.6 4.0 %collective-permute-start.1 = (f32[1,9]{1,0:T(1,128)S(1)}, f32[1,9]{1,0:T(1,128)S(1)}, u32[]{:S(2)}, u32[]{:S(2)}) collective-permute-start(f32[1,9]{1,0:T(1,128)S(1)} %maximum_bitcast_fusion.1), channel_id=1, source_target_pairs={{1,0},{2,1},{3,2},{4,3},{5,4},{6,5},{7,6},{8,7},{9,8},{10,9},{11,1... | collective-permute-start | bytes 116 | tf_op jit(solution)/shard_map/ppermute | solution.py:15
Sparse Core Ops, SparseCore 0:
  13.3 20.9 all-reduce.2
  38.6 70.7 all-reduce.4
where the time goes:
time: 130 us; the launch traced here: 128 us
  waiting for transfers between devices  95.6 us (74%)
  between operations  14.2 us (11%)
  matrix products  9 us (7%)
  local copies, waits for them, and re-layouts  3.46 us (3%)
  other arithmetic  3 us (2%)
  starting transfers between devices  2.64 us (2%)
    psum x1, waiting for transfers between devices, local(): query_grads = lax.psum(partial_grads, 'store')  71.9 us
    psum x1, waiting for transfers between devices, local(): summed = lax.psum(factors, 'mp')  21 us
    dot_general x1, matrix products, local(): jnp.einsum('qtd,kd->qtk', out_grad, proj_out, preferred_element_type=jnp....  3.68 us
    ppermute x1, waiting for transfers between devices, padded_2(): after = lax.ppermute(first, axis, down)  2.71 us
  transfers between devices with their start and end apart: 4, of which 3 were waited for; matrix products, arithmetic and copies ran while one was open for 1% of the time, Pallas kernels for 0%

commit v1 on v0

v1 whole, which is shorter than its diff:
```python
import functools
import math

import jax
import jax.numpy as jnp
from jax import lax
from jax.experimental import pallas as pl
from jax.experimental.pallas import tpu as pltpu
from jax.sharding import PartitionSpec as P

MESH = pl.DeviceIdType.MESH
NT = (((1,), (1,)), ((), ()))
TN = (((0,), (0,)), ((), ()))
EDGE = 64
F32, BF16 = jnp.float32, jnp.bfloat16


def split(value):
    high = value.astype(BF16)
    return high, (value - high.astype(F32)).astype(BF16)


def kernel(
    n, own,
    x_hbm, g_hbm, pi_hbm, po_hbm, cnt, rows_hbm, ids_ref,
    grads_out, rows_out, docs_out,
    x, g, pi, po, rows, fac, peer, gs, part, recv, full, edge_out, edge_in, ext, same,
    load_sem, mp_sem, edge_sem, rs_sem, ag_sem,
):
    queries, span, depth = x_hbm.shape
    half = queries // 2
    ki, ko = pi_hbm.shape[0], po_hbm.shape[0]
    width = ki * ko
    chunk = width // own
    step = n // own
    row_count = rows_hbm.shape[0]
    st, mp = lax.axis_index("store"), lax.axis_index("mp")
    me = st * 2 + mp

    def at(rank):
        return {"store": rank // 2, "mp": lax.rem(rank, 2)}

    def load(src, dst, k):
        copy = pltpu.make_async_copy(src, dst, load_sem.at[k])
        copy.start()
        return copy

    first, second = (1 - mp) * half, mp * half
    loads = [
        load(pi_hbm, pi, 0),
        load(x_hbm.at[pl.ds(first, half)], x.at[pl.ds(0, half)], 1),
        load(po_hbm, po, 2),
        load(g_hbm.at[pl.ds(first, half)], g.at[pl.ds(0, half)], 3),
        load(x_hbm.at[pl.ds(second, half)], x.at[pl.ds(half, half)], 4),
        load(g_hbm.at[pl.ds(second, half)], g.at[pl.ds(half, half)], 5),
        load(rows_hbm, rows, 6),
    ]

    barrier = pltpu.get_barrier_semaphore()

    @pl.loop(1, n)
    def _(k):
        pl.semaphore_signal(barrier, 1, device_id=at(lax.rem(me + k, n)), device_id_type=MESH)

    ids = ids_ref[...].astype(F32)
    across = jnp.broadcast_to(ids, (128, row_count)).T
    for b in range(row_count // 128):
        col = slice(b * 128, (b + 1) * 128)
        same[:, col] = jnp.where(across == ids[:, col], 1.0, 0.0).astype(BF16)

    def factors(h, kx, kg):
        loads[kx].wait()
        xi = x[h * half:(h + 1) * half].reshape(half * span, depth)
        fi = lax.dot_general(xi, pi[...], NT, preferred_element_type=F32)
        loads[kg].wait()
        gi = g[h * half:(h + 1) * half].reshape(half * span, depth)
        fo = lax.dot_general(gi, po[...], NT, preferred_element_type=F32)
        return fi, fo

    loads[0].wait()
    loads[2].wait()
    fi, fo = factors(0, 1, 3)
    fac[...] = jnp.concatenate([fi, fo], axis=1)
    pl.semaphore_wait(barrier, n - 1)
    to_peer = pltpu.make_async_remote_copy(
        src_ref=fac, dst_ref=peer, send_sem=mp_sem.at[0], recv_sem=mp_sem.at[1],
        device_id={"mp": 1 - mp}, device_id_type=MESH,
    )
    to_peer.start()
    fi, fo = factors(1, 4, 5)

    loads[6].wait()
    head_id, tail_id = ids[:, :1], ids[:, row_count - 1:]
    head_mask = jnp.where(ids[:, :EDGE] == head_id, 1.0, 0.0)
    tail_mask = jnp.where(ids[:, row_count - EDGE:] == tail_id, 1.0, 0.0)
    for e, (mask, lo, eid) in enumerate(
        ((head_mask, 0, head_id), (tail_mask, row_count - EDGE, tail_id))
    ):
        wide = jnp.broadcast_to(mask, (16, EDGE)).astype(BF16)
        total = jnp.dot(wide, rows[lo:lo + EDGE, :], preferred_element_type=F32)
        edge_out[e, :, :width] = total[:1]
        edge_out[e, :, width:] = jnp.broadcast_to(eid, (1, 128))
    edges = []
    for e, rank in enumerate((lax.rem(me + n - 1, n), lax.rem(me + 1, n))):
        copy = pltpu.make_async_remote_copy(
            src_ref=edge_out.at[e], dst_ref=edge_in.at[1 - e],
            send_sem=edge_sem.at[e], recv_sem=edge_sem.at[3 - e],
            device_id=at(rank), device_id_type=MESH,
        )
        copy.start()
        edges.append(copy)

    to_peer.wait_recv()
    fi = fi + peer[:, :ki]
    fo = fo + peer[:, ki:]
    pos = st * span + lax.broadcasted_iota(jnp.int32, (span, ko), 0)
    for k in range(half):
        count = cnt[second + k]
        weight = jnp.where(pos < count, 1.0, 0.0) / jnp.full((span, ko), count, jnp.int32).astype(F32)
        a_hi, a_lo = split(fo[k * span:(k + 1) * span] * weight)
        b_hi, b_lo = split(fi[k * span:(k + 1) * span])
        lhs = jnp.concatenate([a_hi, a_hi, a_lo], axis=0)
        rhs = jnp.concatenate([b_hi, b_lo, b_hi], axis=0)
        outer = lax.dot_general(lhs, jnp.concatenate([rhs, rhs], axis=1), TN, preferred_element_type=F32)
        gs[k * ko:(k + 1) * ko, :] = outer
    lower = lax.broadcasted_iota(jnp.int32, (half, 128), 1) < ki
    for j in range(width // 128):
        even = gs[pl.ds(2 * j, half, stride=ko), :]
        odd = gs[pl.ds(2 * j + 1, half, stride=ko), :]
        c, off = divmod(j * 128, chunk)
        part[c, :, off:off + 128] = jnp.where(lower, even, odd)

    mine = me // step
    is_owner = lax.rem(me, step) == 0

    def guarded(cond, fn):
        if own == n:
            fn()
        else:
            pl.when(cond)(fn)

    @pl.loop(1 if own == n else 0, own)
    def _(k):
        c = lax.rem(mine + k, own)
        rank = c * step

        def send():
            pltpu.make_async_remote_copy(
                src_ref=part.at[c], dst_ref=recv.at[me], send_sem=rs_sem.at[0],
                recv_sem=rs_sem.at[1], device_id=at(rank), device_id_type=MESH,
            ).start()

        guarded(rank != me, send)

    def drain(buf, count, sem):
        view = buf.at[pl.ds(0, count)]
        pltpu.make_async_copy(view, view, sem).wait()

    def combine():
        recv[me] = part[mine]
        drain(recv, n - 1, rs_sem.at[1])
        sums = []
        for m in range(2):
            total = recv[m]
            for s in range(1, n // 2):
                total = total + recv[2 * s + m]
            sums.append(total)
        full[mine] = jnp.concatenate(sums, axis=0)

        @pl.loop(1, n)
        def _(k):
            pltpu.make_async_remote_copy(
                src_ref=full.at[mine], dst_ref=full.at[mine], send_sem=ag_sem.at[0],
                recv_sem=ag_sem.at[1], device_id=at(lax.rem(me + k, n)), device_id_type=MESH,
            ).start()

    guarded(is_owner, combine)

    for copy in edges:
        copy.wait_recv()
    l_hi, l_lo = split(edge_in[0, :, :width])
    r_hi, r_lo = split(edge_in[1, :, :width])
    left_id = jnp.where(me == 0, -1.0, edge_in[0, :, width:width + 1])
    right_id = jnp.where(me == n - 1, -1.0, edge_in[1, :, width:width + 1])
    line = lax.broadcasted_iota(jnp.int32, (16, width), 0)
    stack = jnp.zeros((16, width), F32)
    for e, term in enumerate((l_hi, l_lo, r_hi, r_lo)):
        stack = jnp.where(line == e, term.astype(F32), stack)
    ext[...] = stack.astype(BF16)

    guarded(is_owner, lambda: drain(full, own - 1, ag_sem.at[1]))
    if own != n:
        pl.when(jnp.logical_not(is_owner))(lambda: drain(full, own, ag_sem.at[1]))

    grads = jnp.concatenate([full[c] for c in range(own)], axis=1)
    grads_out[...] = grads
    low = grads.astype(BF16)
    scores = lax.dot_general(low, rows[...], NT, preferred_element_type=F32)
    around = lax.dot_general(low, ext[...], NT, preferred_element_type=F32)
    rows_out[...] = scores
    s_hi, s_lo = split(scores)
    docs = jnp.dot(s_hi, same[...], preferred_element_type=F32) + jnp.dot(
        s_lo, same[...], preferred_element_type=F32
    )
    docs = docs + jnp.where(ids == left_id, around[:, 0:1] + around[:, 1:2], 0.0)
    docs = docs + jnp.where(ids == right_id, around[:, 2:3] + around[:, 3:4], 0.0)
    docs_out[...] = docs

    to_peer.wait_send()
    for copy in edges:
        copy.wait_send()
    if own == n:
        drain(part, own - 1, rs_sem.at[0])
        drain(full, n - 1, ag_sem.at[0])
    else:
        @pl.when(is_owner)
        def _():
            drain(part, own - 1, rs_sem.at[0])
            for _ in range((n - 1) // (own - 1)):
                drain(full, own - 1, ag_sem.at[0])
            if (n - 1) % (own - 1):
                drain(full, (n - 1) % (own - 1), ag_sem.at[0])

        @pl.when(jnp.logical_not(is_owner))
        def _():
            drain(part, own, rs_sem.at[0])


def local(layer_input, out_grad, proj_in, proj_out, counts, store_rows, doc_ids):
    n = lax.axis_size("store") * lax.axis_size("mp")
    queries, span, depth = layer_input.shape
    half = queries // 2
    ki, ko = proj_in.shape[0], proj_out.shape[0]
    width = ki * ko
    own = math.gcd(n, width // 128)
    chunk = width // own
    row_count = store_rows.shape[0]
    hbm = pl.BlockSpec(memory_space=pl.ANY)
    vmem = pl.BlockSpec(memory_space=pltpu.VMEM)
    smem = pl.BlockSpec(memory_space=pltpu.SMEM)
    return pl.pallas_call(
        functools.partial(kernel, n, own),
        out_shape=(
            jax.ShapeDtypeStruct((queries, width), F32),
            jax.ShapeDtypeStruct((queries, row_count), F32),
            jax.ShapeDtypeStruct((queries, row_count), F32),
        ),
        in_specs=[hbm, hbm, hbm, hbm, smem, hbm, vmem],
        out_specs=(vmem, vmem, vmem),
        scratch_shapes=[
            pltpu.VMEM(layer_input.shape, BF16),
            pltpu.VMEM(out_grad.shape, BF16),
            pltpu.VMEM(proj_in.shape, BF16),
            pltpu.VMEM(proj_out.shape, BF16),
            pltpu.VMEM(store_rows.shape, BF16),
            pltpu.VMEM((half * span, ki + ko), F32),
            pltpu.VMEM((half * span, ki + ko), F32),
            pltpu.VMEM((half * ko, 2 * ki), F32),
            pltpu.VMEM((own, half, chunk), F32),
            pltpu.VMEM((n, half, chunk), F32),
            pltpu.VMEM((own, queries, chunk), F32),
            pltpu.VMEM((2, 1, width + 128), F32),
            pltpu.VMEM((2, 1, width + 128), F32),
            pltpu.VMEM((16, width), BF16),
            pltpu.VMEM((row_count, row_count), BF16),
            pltpu.SemaphoreType.DMA((7,)),
            pltpu.SemaphoreType.DMA((2,)),
            pltpu.SemaphoreType.DMA((4,)),
            pltpu.SemaphoreType.DMA((2,)),
            pltpu.SemaphoreType.DMA((2,)),
        ],
        compiler_params=pltpu.CompilerParams(
            collective_id=0, has_side_effects=True, vmem_limit_bytes=62 * 1024 * 1024
        ),
    )(layer_input, out_grad, proj_in, proj_out, counts, store_rows, doc_ids.reshape(1, -1))


def solution(mesh):
    placed = (
        P("dom", "store", "mp"),
        P("dom", "store", "mp"),
        P(None, "mp"),
        P(None, "mp"),
        P("dom"),
        P(("dom", "store", "mp"), None),
        P(("dom", "store", "mp")),
    )
    return jax.shard_map(
        local,
        mesh=mesh,
        in_specs=placed,
        out_specs=(P("dom", None), P("dom", ("store", "mp")), P("dom", ("store", "mp"))),
        check_vma=False,
    )
```

time: 130 us -> 27.4 us (0.21); the launches traced: 128 us -> 27.1 us
  waiting for transfers between devices: 95.6 us -> 0 us
  Pallas kernels: 0 us -> 21 us
  between operations: 14.2 us -> 0.64 us
  matrix products: 9 us -> 0 us
  other arithmetic: 3 us -> 0 us
  starting transfers between devices: 2.64 us -> 0 us
  local copies, waits for them, and re-layouts: 3.46 us -> 5.43 us
    psum x2 -> x0, waiting for transfers between devices: 92.8 us -> none  [the longest x1 71.9 us: local(): query_grads = lax.psum(partial_grads, 'store')]
    pallas_call x0 -> x1, Pallas kernels: none -> 21 us  [local(): pl.pallas_call(functools.partial(kernel, n, own), out_shape=(jax.ShapeDty...]
    dot_general x5 -> x0, matrix products: 9 us -> none  [the longest x1 3.68 us: local(): jnp.einsum('qtd,kd->qtk', out_grad, proj_out, preferred_element_type=jnp....]
    ppermute x2 -> x0, waiting for transfers between devices: 2.72 us -> none  [the longest x1 2.71 us: padded_2(): after = lax.ppermute(first, axis, down)]
    ppermute x2 -> x0, starting transfers between devices: 2.56 us -> none  [the longest x1 1.28 us: padded_2(): after = lax.ppermute(first, axis, down)]
    unnamed x13 -> x3, local copies, waits for them, and re-layouts: 1.75 us -> 4.18 us
    another operation x2 -> x0, other arithmetic: 1.36 us -> none  [local(): summary = jnp.stack([head_entry, tail_entry])]
  transfers between devices with their start and end apart: 4 -> 0, of which waited for: 3 -> 0; matrix products, arithmetic and copies ran while one was open for 1% -> 0% of each run, Pallas kernels for 0% -> 0%
where the time goes in v1:
time: 27.4 us; the launch traced here: 27.1 us
  Pallas kernels  21 us (77%)
  local copies, waits for them, and re-layouts  5.43 us (20%)
  between operations  0.64 us (2%)
    pallas_call x1, Pallas kernels, local(): pl.pallas_call(functools.partial(kernel, n, own), out_shape=(jax.ShapeDty...  21 us
    unnamed x3, local copies, waits for them, and re-layouts  4.18 us
    reshape x1, local copies, waits for them, and re-layouts, local(): doc_ids.reshape(1, -1)  1.25 us

profile of v1, /device:TPU:0, one launch (start us, length us, event | category | flops | bytes accessed | tf_op | source)
XLA Modules:
  0.0 27.1 jit_solution(894577803969202071)
XLA Ops:
  0.6 1.2 %reshape.9.ids_ref = s32[1,384]{1,0:T(1,128)} reshape(s32[384]{0:T(512)} %param.13) | data formatting | bytes 3072 | tf_op jit(solution)/shard_map/reshape | solution.py:275
  1.9 21.0 %shard_map.94 = (f32[8,4096]{1,0:T(8,128)}, f32[8,384]{1,0:T(8,128)}, f32[8,384]{1,0:T(8,128)}) custom-call(bf16[8,64,4096]{2,1,0:T(8,128)(2,1)} %x_hbm.1, bf16[8,64,4096]{2,1,0:T(8,128)(2,1)} %g_hbm.1, bf16[64,4096]{1,0:T(8,128)(2,1)} %pi_hbm.1, bf16[64,4096]{1,0:T(8,128)(2,1)} %po_hbm.1, s32[8]{0:T(128)} %cnt.1, bf16[384,4096]{1,0:T(8,128)(2,1)} %rows_hbm.1, ...), custom_call_target="tpu_custom_call" | custom-call | tf_op jit(solution)/shard_map/pallas_call | solution.py:241
  22.9 1.6 %copy.13 = f32[8,4096]{1,0:T(8,128)} copy(f32[8,4096]{1,0:T(8,128)} %get-tuple-element.6) | data formatting | bytes 262144
  24.5 1.3 %copy.14 = f32[8,384]{1,0:T(8,128)} copy(f32[8,384]{1,0:T(8,128)} %get-tuple-element.7) | data formatting | bytes 24576
  25.8 1.3 %copy.15 = f32[8,384]{1,0:T(8,128)} copy(f32[8,384]{1,0:T(8,128)} %get-tuple-element.8) | data formatting | bytes 24576

commit v2 on v1

--- a/solution.py
+++ b/solution.py
@@ -23,7 +23,7 @@
 def kernel(
     n, own,
     x_hbm, g_hbm, pi_hbm, po_hbm, cnt, rows_hbm, ids_ref,
-    grads_out, rows_out, docs_out,
+    out,
     x, g, pi, po, rows, fac, peer, gs, part, recv, full, edge_out, edge_in, ext, same,
     load_sem, mp_sem, edge_sem, rs_sem, ag_sem,
 ):
@@ -53,7 +53,6 @@
         load(g_hbm.at[pl.ds(first, half)], g.at[pl.ds(0, half)], 3),
         load(x_hbm.at[pl.ds(second, half)], x.at[pl.ds(half, half)], 4),
         load(g_hbm.at[pl.ds(second, half)], g.at[pl.ds(half, half)], 5),
-        load(rows_hbm, rows, 6),
     ]
 
     barrier = pltpu.get_barrier_semaphore()
@@ -62,7 +61,7 @@
     def _(k):
         pl.semaphore_signal(barrier, 1, device_id=at(lax.rem(me + k, n)), device_id_type=MESH)
 
-    ids = ids_ref[...].astype(F32)
+    ids = ids_ref[...].astype(F32).reshape(1, row_count)
     across = jnp.broadcast_to(ids, (128, row_count)).T
     for b in range(row_count // 128):
         col = slice(b * 128, (b + 1) * 128)
@@ -87,7 +86,50 @@
         device_id={"mp": 1 - mp}, device_id_type=MESH,
     )
     to_peer.start()
+    loads.append(load(rows_hbm, rows, 6))
     fi, fo = factors(1, 4, 5)
+
+    to_peer.wait_recv()
+    fi = fi + peer[:, :ki]
+    fo = fo + peer[:, ki:]
+    pos = st * span + lax.broadcasted_iota(jnp.int32, (span, ko), 0)
+    for k in range(half):
+        count = cnt[second + k]
+        weight = jnp.where(pos < count, 1.0, 0.0) / jnp.full((span, ko), count, jnp.int32).astype(F32)
+        a_hi, a_lo = split(fo[k * span:(k + 1) * span] * weight)
+        b_hi, b_lo = split(fi[k * span:(k + 1) * span])
+        lhs = jnp.concatenate([a_hi, a_hi, a_lo], axis=0)
+        rhs = jnp.concatenate([b_hi, b_lo, b_hi], axis=0)
+        outer = lax.dot_general(lhs, jnp.concatenate([rhs, rhs], axis=1), TN, preferred_element_type=F32)
+        gs[k * ko:(k + 1) * ko, :] = outer
+    lower = lax.broadcasted_iota(jnp.int32, (half, 128), 1) < ki
+    for j in range(width // 128):
+        even = gs[pl.ds(2 * j, half, stride=ko), :]
+        odd = gs[pl.ds(2 * j + 1, half, stride=ko), :]
+        c, off = divmod(j * 128, chunk)
+        part[c, :, off:off + 128] = jnp.where(lower, even, odd)
+
+    mine = me // step
+    is_owner = lax.rem(me, step) == 0
+
+    def guarded(cond, fn):
+        if own == n:
+            fn()
+        else:
+            pl.when(cond)(fn)
+
+    @pl.loop(1 if own == n else 0, own)
+    def _(k):
+        c = lax.rem(mine + k, own)
+        rank = c * step
+
+        def send():
+            pltpu.make_async_remote_copy(
+                src_ref=part.at[c], dst_ref=recv.at[me], send_sem=rs_sem.at[0],
+                recv_sem=rs_sem.at[1], device_id=at(rank), device_id_type=MESH,
+            ).start()
+
+        guarded(rank != me, send)
 
     loads[6].wait()
     head_id, tail_id = ids[:, :1], ids[:, row_count - 1:]
@@ -110,48 +152,6 @@
         copy.start()
         edges.append(copy)
 
-    to_peer.wait_recv()
-    fi = fi + peer[:, :ki]
-    fo = fo + peer[:, ki:]
-    pos = st * span + lax.broadcasted_iota(jnp.int32, (span, ko), 0)
-    for k in range(half):
-        count = cnt[second + k]
-        weight = jnp.where(pos < count, 1.0, 0.0) / jnp.full((span, ko), count, jnp.int32).astype(F32)
-        a_hi, a_lo = split(fo[k * span:(k + 1) * span] * weight)
-        b_hi, b_lo = split(fi[k * span:(k + 1) * span])
-        lhs = jnp.concatenate([a_hi, a_hi, a_lo], axis=0)
-        rhs = jnp.concatenate([b_hi, b_lo, b_hi], axis=0)
-        outer = lax.dot_general(lhs, jnp.concatenate([rhs, rhs], axis=1), TN, preferred_element_type=F32)
-        gs[k * ko:(k + 1) * ko, :] = outer
-    lower = lax.broadcasted_iota(jnp.int32, (half, 128), 1) < ki
-    for j in range(width // 128):
-        even = gs[pl.ds(2 * j, half, stride=ko), :]
-        odd = gs[pl.ds(2 * j + 1, half, stride=ko), :]
-        c, off = divmod(j * 128, chunk)
-        part[c, :, off:off + 128] = jnp.where(lower, even, odd)
-
-    mine = me // step
-    is_owner = lax.rem(me, step) == 0
-
-    def guarded(cond, fn):
-        if own == n:
-            fn()
-        else:
-            pl.when(cond)(fn)
-
-    @pl.loop(1 if own == n else 0, own)
-    def _(k):
-        c = lax.rem(mine + k, own)
-        rank = c * step
-
-        def send():
-            pltpu.make_async_remote_copy(
-                src_ref=part.at[c], dst_ref=recv.at[me], send_sem=rs_sem.at[0],
-                recv_sem=rs_sem.at[1], device_id=at(rank), device_id_type=MESH,
-            ).start()
-
-        guarded(rank != me, send)
-
     def drain(buf, count, sem):
         view = buf.at[pl.ds(0, count)]
         pltpu.make_async_copy(view, view, sem).wait()
@@ -193,18 +193,18 @@
         pl.when(jnp.logical_not(is_owner))(lambda: drain(full, own, ag_sem.at[1]))
 
     grads = jnp.concatenate([full[c] for c in range(own)], axis=1)
-    grads_out[...] = grads
+    out[:, :width] = grads
     low = grads.astype(BF16)
     scores = lax.dot_general(low, rows[...], NT, preferred_element_type=F32)
     around = lax.dot_general(low, ext[...], NT, preferred_element_type=F32)
-    rows_out[...] = scores
+    out[:, width:width + row_count] = scores
     s_hi, s_lo = split(scores)
     docs = jnp.dot(s_hi, same[...], preferred_element_type=F32) + jnp.dot(
         s_lo, same[...], preferred_element_type=F32
     )
     docs = docs + jnp.where(ids == left_id, around[:, 0:1] + around[:, 1:2], 0.0)
     docs = docs + jnp.where(ids == right_id, around[:, 2:3] + around[:, 3:4], 0.0)
-    docs_out[...] = docs
+    out[:, width + row_count:] = docs
 
     to_peer.wait_send()
     for copy in edges:
@@ -226,6 +226,30 @@
             drain(part, own, rs_sem.at[0])
 
 
+def parts(joined, grads_out, rows_out, docs_out, sem):
+    at = 0
+    copies = []
+    for k, out in enumerate((grads_out, rows_out, docs_out)):
+        width = out.shape[1]
+        copies.append(pltpu.make_async_copy(joined.at[:, at:at + width], out, sem.at[k]))
+        copies[-1].start()
+        at += width
+    for copy in copies:
+        copy.wait()
+
+
+def hand_out(joined, width, row_count):
+    queries = joined.shape[0]
+    widths = (width, row_count, row_count)
+    return pl.pallas_call(
+        parts,
+        out_shape=tuple(jax.ShapeDtypeStruct((queries, w), F32) for w in widths),
+        in_specs=[pl.BlockSpec(memory_space=pltpu.VMEM)],
+        out_specs=tuple(pl.BlockSpec(memory_space=pl.ANY) for _ in widths),
+        scratch_shapes=[pltpu.SemaphoreType.DMA((3,))],
+    )(joined)
+
+
 def local(layer_input, out_grad, proj_in, proj_out, counts, store_rows, doc_ids):
     n = lax.axis_size("store") * lax.axis_size("mp")
     queries, span, depth = layer_input.shape
@@ -238,15 +262,11 @@
     hbm = pl.BlockSpec(memory_space=pl.ANY)
     vmem = pl.BlockSpec(memory_space=pltpu.VMEM)
     smem = pl.BlockSpec(memory_space=pltpu.SMEM)
-    return pl.pallas_call(
+    joined = pl.pallas_call(
         functools.partial(kernel, n, own),
-        out_shape=(
-            jax.ShapeDtypeStruct((queries, width), F32),
-            jax.ShapeDtypeStruct((queries, row_count), F32),
-            jax.ShapeDtypeStruct((queries, row_count), F32),
-        ),
+        out_shape=jax.ShapeDtypeStruct((queries, width + 2 * row_count), F32),
         in_specs=[hbm, hbm, hbm, hbm, smem, hbm, vmem],
-        out_specs=(vmem, vmem, vmem),
+        out_specs=vmem,
         scratch_shapes=[
             pltpu.VMEM(layer_input.shape, BF16),
             pltpu.VMEM(out_grad.shape, BF16),
@@ -272,7 +292,8 @@
         compiler_params=pltpu.CompilerParams(
             collective_id=0, has_side_effects=True, vmem_limit_bytes=62 * 1024 * 1024
         ),
-    )(layer_input, out_grad, proj_in, proj_out, counts, store_rows, doc_ids.reshape(1, -1))
+    )(layer_input, out_grad, proj_in, proj_out, counts, store_rows, doc_ids)
+    return hand_out(joined, width, row_count)
 
 
 def solution(mesh):

time: 27.4 us -> 23.4 us (0.85)
  local copies, waits for them, and re-layouts: 5.43 us -> 0 us
  Pallas kernels: 21 us -> 22.6 us
    unnamed x3 -> x0, local copies, waits for them, and re-layouts: 4.18 us -> none
    pallas_call x1 -> x2, Pallas kernels: 21 us -> 22.6 us  [the longest x1 21 us: local(): pl.pallas_call(functools.partial(kernel, n, own), out_shape=jax.ShapeDtyp...]
    reshape x1 -> x0, local copies, waits for them, and re-layouts: 1.25 us -> none  [local(): doc_ids.reshape(1, -1)]
where the time goes in v2:
time: 23.4 us; the launch traced here: 23.2 us
  Pallas kernels  22.6 us (97%)
  between operations  0.64 us (3%)
    pallas_call x1, Pallas kernels, local(): pl.pallas_call(functools.partial(kernel, n, own), out_shape=jax.ShapeDtyp...  21 us
    pallas_call x1, Pallas kernels, hand_out(): pl.pallas_call(parts, out_shape=tuple((jax.ShapeDtypeStruct((queries, w),...  1.6 us

profile of v2, /device:TPU:0, one launch (start us, length us, event | category | flops | bytes accessed | tf_op | source)
XLA Modules:
  0.0 23.2 jit_solution(12568706253454238892)
XLA Ops:
  0.6 21.0 %shard_map.94.joined = f32[8,4864]{1,0:T(8,128)} custom-call(bf16[8,64,4096]{2,1,0:T(8,128)(2,1)} %x_hbm.1, bf16[8,64,4096]{2,1,0:T(8,128)(2,1)} %g_hbm.1, bf16[64,4096]{1,0:T(8,128)(2,1)} %pi_hbm.1, bf16[64,4096]{1,0:T(8,128)(2,1)} %po_hbm.1, s32[8]{0:T(128)} %cnt.1, bf16[384,4096]{1,0:T(8,128)(2,1)} %rows_hbm.1, s32[384]{0:T(512)} %ids_ref.1), custom_call_target="tpu_custom_call" | custom-call | tf_op jit(solution)/shard_map/pallas_call | solution.py:265
  21.6 1.6 %shard_map.95 = (f32[8,4096]{1,0:T(8,128)}, f32[8,384]{1,0:T(8,128)}, f32[8,384]{1,0:T(8,128)}) custom-call(f32[8,4864]{1,0:T(8,128)} %shard_map.94.joined), custom_call_target="tpu_custom_call" | custom-call | tf_op jit(solution)/shard_map/pallas_call | solution.py:244

commit v3 on v2

--- a/solution.py
+++ b/solution.py
@@ -25,7 +25,7 @@
     x_hbm, g_hbm, pi_hbm, po_hbm, cnt, rows_hbm, ids_ref,
     out,
     x, g, pi, po, rows, fac, peer, gs, part, recv, full, edge_out, edge_in, ext, same,
-    load_sem, mp_sem, edge_sem, rs_sem, ag_sem,
+    load_sem, mp_sem, edge_sem, rs_sem, ag_sem, slot_sem,
 ):
     queries, span, depth = x_hbm.shape
     half = queries // 2
@@ -46,14 +46,12 @@
         return copy
 
     first, second = (1 - mp) * half, mp * half
-    loads = [
-        load(pi_hbm, pi, 0),
-        load(x_hbm.at[pl.ds(first, half)], x.at[pl.ds(0, half)], 1),
-        load(po_hbm, po, 2),
-        load(g_hbm.at[pl.ds(first, half)], g.at[pl.ds(0, half)], 3),
-        load(x_hbm.at[pl.ds(second, half)], x.at[pl.ds(half, half)], 4),
-        load(g_hbm.at[pl.ds(second, half)], g.at[pl.ds(half, half)], 5),
-    ]
+    loads = {"pi": load(pi_hbm, pi, 0), "po": load(po_hbm, po, 1)}
+    pair = half // 2
+    for b in range(4):
+        start = (first, second)[b // 2] + b % 2 * pair
+        for k, (src, dst) in enumerate(((x_hbm, x), (g_hbm, g))):
+            loads[b, k] = load(src.at[pl.ds(start, pair)], dst.at[pl.ds(b * pair, pair)], 2 + 2 * b + k)
 
     barrier = pltpu.get_barrier_semaphore()
 
@@ -67,18 +65,18 @@
         col = slice(b * 128, (b + 1) * 128)
         same[:, col] = jnp.where(across == ids[:, col], 1.0, 0.0).astype(BF16)
 
-    def factors(h, kx, kg):
-        loads[kx].wait()
-        xi = x[h * half:(h + 1) * half].reshape(half * span, depth)
-        fi = lax.dot_general(xi, pi[...], NT, preferred_element_type=F32)
-        loads[kg].wait()
-        gi = g[h * half:(h + 1) * half].reshape(half * span, depth)
-        fo = lax.dot_general(gi, po[...], NT, preferred_element_type=F32)
-        return fi, fo
-
-    loads[0].wait()
-    loads[2].wait()
-    fi, fo = factors(0, 1, 3)
+    def factors(h):
+        terms = [[], []]
+        for b in (2 * h, 2 * h + 1):
+            for k, (act, proj) in enumerate(((x, pi), (g, po))):
+                loads[b, k].wait()
+                block = act[b * pair:(b + 1) * pair].reshape(pair * span, depth)
+                terms[k].append(lax.dot_general(block, proj[...], NT, preferred_element_type=F32))
+        return [jnp.concatenate(t, axis=0) for t in terms]
+
+    loads["pi"].wait()
+    loads["po"].wait()
+    fi, fo = factors(0)
     fac[...] = jnp.concatenate([fi, fo], axis=1)
     pl.semaphore_wait(barrier, n - 1)
     to_peer = pltpu.make_async_remote_copy(
@@ -86,8 +84,8 @@
         device_id={"mp": 1 - mp}, device_id_type=MESH,
     )
     to_peer.start()
-    loads.append(load(rows_hbm, rows, 6))
-    fi, fo = factors(1, 4, 5)
+    loads["rows"] = load(rows_hbm, rows, 10)
+    fi, fo = factors(1)
 
     to_peer.wait_recv()
     fi = fi + peer[:, :ki]
@@ -131,7 +129,7 @@
 
         guarded(rank != me, send)
 
-    loads[6].wait()
+    loads["rows"].wait()
     head_id, tail_id = ids[:, :1], ids[:, row_count - 1:]
     head_mask = jnp.where(ids[:, :EDGE] == head_id, 1.0, 0.0)
     tail_mask = jnp.where(ids[:, row_count - EDGE:] == tail_id, 1.0, 0.0)
@@ -171,7 +169,7 @@
         def _(k):
             pltpu.make_async_remote_copy(
                 src_ref=full.at[mine], dst_ref=full.at[mine], send_sem=ag_sem.at[0],
-                recv_sem=ag_sem.at[1], device_id=at(lax.rem(me + k, n)), device_id_type=MESH,
+                recv_sem=slot_sem.at[me] if own == n else ag_sem.at[1], device_id=at(lax.rem(me + k, n)), device_id_type=MESH,
             ).start()
 
     guarded(is_owner, combine)
@@ -188,15 +186,35 @@
         stack = jnp.where(line == e, term.astype(F32), stack)
     ext[...] = stack.astype(BF16)
 
-    guarded(is_owner, lambda: drain(full, own - 1, ag_sem.at[1]))
-    if own != n:
+    if own == n:
+        scores = jnp.zeros((queries, row_count), F32)
+        around = jnp.zeros((queries, 16), F32)
+        for k in range(n // 2):
+            s = lax.rem(st - k + n // 2, n // 2)
+            for m in range(2):
+                c = 2 * s + m
+
+                def land():
+                    pltpu.make_async_copy(full.at[c], full.at[c], slot_sem.at[c]).wait()
+
+                if k == 0:
+                    pl.when(mp != m)(land)
+                else:
+                    land()
+            grads = jnp.concatenate([full[2 * s], full[2 * s + 1]], axis=1)
+            cols = pl.ds(pl.multiple_of(s * (2 * chunk), 2 * chunk), 2 * chunk)
+            out[:, cols] = grads
+            low = grads.astype(BF16)
+            scores += lax.dot_general(low, rows[:, cols], NT, preferred_element_type=F32)
+            around += lax.dot_general(low, ext[:, cols], NT, preferred_element_type=F32)
+    else:
+        pl.when(is_owner)(lambda: drain(full, own - 1, ag_sem.at[1]))
         pl.when(jnp.logical_not(is_owner))(lambda: drain(full, own, ag_sem.at[1]))
-
-    grads = jnp.concatenate([full[c] for c in range(own)], axis=1)
-    out[:, :width] = grads
-    low = grads.astype(BF16)
-    scores = lax.dot_general(low, rows[...], NT, preferred_element_type=F32)
-    around = lax.dot_general(low, ext[...], NT, preferred_element_type=F32)
+        grads = jnp.concatenate([full[c] for c in range(own)], axis=1)
+        out[:, :width] = grads
+        low = grads.astype(BF16)
+        scores = lax.dot_general(low, rows[...], NT, preferred_element_type=F32)
+        around = lax.dot_general(low, ext[...], NT, preferred_element_type=F32)
     out[:, width:width + row_count] = scores
     s_hi, s_lo = split(scores)
     docs = jnp.dot(s_hi, same[...], preferred_element_type=F32) + jnp.dot(
@@ -283,11 +301,12 @@
             pltpu.VMEM((2, 1, width + 128), F32),
             pltpu.VMEM((16, width), BF16),
             pltpu.VMEM((row_count, row_count), BF16),
-            pltpu.SemaphoreType.DMA((7,)),
+            pltpu.SemaphoreType.DMA((11,)),
             pltpu.SemaphoreType.DMA((2,)),
             pltpu.SemaphoreType.DMA((4,)),
             pltpu.SemaphoreType.DMA((2,)),
             pltpu.SemaphoreType.DMA((2,)),
+            pltpu.SemaphoreType.DMA((n,)),
         ],
         compiler_params=pltpu.CompilerParams(
             collective_id=0, has_side_effects=True, vmem_limit_bytes=62 * 1024 * 1024

time: 23.4 us -> 22.9 us (0.979)
  Pallas kernels: 22.6 us -> 22.1 us
    pallas_call x1, Pallas kernels: 21 us -> 20.5 us  [local(): pl.pallas_call(functools.partial(kernel, n, own), out_shape=jax.ShapeDtyp...]
where the time goes in v3:
time: 22.9 us; the launch traced here: 22.8 us
  Pallas kernels  22.1 us (97%)
  between operations  0.64 us (3%)
    pallas_call x1, Pallas kernels, local(): pl.pallas_call(functools.partial(kernel, n, own), out_shape=jax.ShapeDtyp...  20.5 us
    pallas_call x1, Pallas kernels, hand_out(): pl.pallas_call(parts, out_shape=tuple((jax.ShapeDtypeStruct((queries, w),...  1.6 us

profile of v3, /device:TPU:0, one launch (start us, length us, event | category | flops | bytes accessed | tf_op | source)
XLA Modules:
  0.0 22.8 jit_solution(9991777889475488789)
XLA Ops:
  0.6 20.5 %shard_map.94.joined = f32[8,4864]{1,0:T(8,128)} custom-call(bf16[8,64,4096]{2,1,0:T(8,128)(2,1)} %x_hbm.1, bf16[8,64,4096]{2,1,0:T(8,128)(2,1)} %g_hbm.1, bf16[64,4096]{1,0:T(8,128)(2,1)} %pi_hbm.1, bf16[64,4096]{1,0:T(8,128)(2,1)} %po_hbm.1, s32[8]{0:T(128)} %cnt.1, bf16[384,4096]{1,0:T(8,128)(2,1)} %rows_hbm.1, s32[384]{0:T(512)} %ids_ref.1), custom_call_target="tpu_custom_call" | custom-call | tf_op jit(solution)/shard_map/pallas_call | solution.py:283
  21.2 1.6 %shard_map.95 = (f32[8,4096]{1,0:T(8,128)}, f32[8,384]{1,0:T(8,128)}, f32[8,384]{1,0:T(8,128)}) custom-call(f32[8,4864]{1,0:T(8,128)} %shard_map.94.joined), custom_call_target="tpu_custom_call" | custom-call | tf_op jit(solution)/shard_map/pallas_call | solution.py:262
